TPU v7x, 256 devices: a whole 4x4x8 slice. The times are simulated.
256 devices in a mesh: seq: 16 (over z, core), chan: 16 (over x, y).
Axes of the slice: x: 4, y: 4, z: 8, core: 2. Of those that a mesh axis runs over, the one named last changes fastest.
Arguments:
- x_groups: bfloat16 [32, 128, 4096], P('seq', None, 'chan'), may hold values from -6 to 6
- grad_groups: bfloat16 [32, 128, 4096], P('seq', None, 'chan'), may hold values from -0.09375 to 0.09375
- filters: bfloat16 [4096, 4096], P('seq', 'chan'), may hold values from -6 to 6
- group_order: int32 [32], replicated, may hold values from 0 to 31, each once
Outputs:
- grad_x: bfloat16 [32, 128, 4096], P('seq', None, 'chan')
- grad_filters: float32 [4096, 4096], P('seq', 'chan')
Inputs may be any that keep to these rules, and one draw needn't show every extreme that they name: `group_order`: a permutation of the 32 block numbers.
All inputs are finite; a program needn't handle non-finite values.
Results may differ from a plain program's by a relative error of at most 0.001.
Values may be sent and summed in bfloat16 or wider, within the bound.
No kernel may reach another device: no remote copies, remote signals or barrier semaphores. Data moves between devices by JAX's collectives and lax.ppermute only.
A program may use at most 128 MiB of HBM per device.

v0:
```python
import functools

import jax
import jax.numpy as jnp
from jax import lax
from jax.experimental import pallas as pl
from jax.experimental.pallas import tpu as pltpu
from jax.sharding import PartitionSpec as P

VMEM_LIMIT = 48 * 1024 * 1024
UNROLL = 8
CODE_SCALE = 2.0**30


def permuter(size, flip):
    rows = lax.broadcasted_iota(jnp.int32, (size, size), 0)
    cols = lax.broadcasted_iota(jnp.int32, (size, size), 1)
    if flip:
        cols = size - 1 - cols
    return (rows == cols).astype(jnp.float32).astype(jnp.bfloat16)


def transposed(eye, value):
    return lax.dot_general(
        eye, value, (((1,), (1,)), ((), ())), preferred_element_type=jnp.float32
    )


def pack_kernel(x_hbm, g_hbm, h_hbm, out_ref, x_ref, g_ref, h_ref, sems):
    peers, _, blocks, part, rows = out_ref.shape
    channels = peers * part
    copies = [
        pltpu.make_async_copy(source, target, sems.at[i])
        for i, (source, target) in enumerate(
            ((g_hbm, g_ref), (x_hbm, x_ref), (h_hbm, h_ref))
        )
    ]
    for copy in copies:
        copy.start()
    flip = permuter(rows, True)

    def put(a, b, value):
        out_ref[:, a, b] = value.astype(jnp.bfloat16).reshape(peers, part, rows)

    copies[0].wait()
    for b in range(blocks):
        put(1, b, jnp.dot(g_ref[b].T, flip, preferred_element_type=jnp.float32))
    copies[1].wait()
    for b in range(blocks):
        put(0, b, x_ref[b].T)
    copies[2].wait()
    for b in range(blocks):
        put(2, b, h_ref[b * rows : (b + 1) * rows, :].T)


def unpack_kernel(in_ref, gx_ref, gf_ref):
    peers, _, blocks, part, rows = in_ref.shape
    channels = peers * part
    eye = permuter(rows, True)
    for b in range(blocks):
        cube = transposed(eye, in_ref[:, 0, b].reshape(channels, rows))
        dx = in_ref[:, 1, b].reshape(channels, rows)
        size = jnp.exp2(jnp.log2(jnp.abs(cube)) * (1.0 / 3.0)) * (1.0 / CODE_SCALE)
        size = jnp.where(cube == 0.0, 0.0, size)
        gf_ref[b * rows : (b + 1) * rows, :] = jnp.where(cube < 0.0, -size, size)
        gx_ref[b] = transposed(eye, dx).astype(jnp.bfloat16)


def conv_kernel(order_ref, in_ref, out_ref, xs, seq, ub, res, wbuf, abuf):
    f32, bf16 = jnp.float32, jnp.bfloat16
    peers, _, blocks, part, rows = in_ref.shape
    total = peers * blocks
    fine = 16
    coarse = rows // fine
    groups = total // coarse

    def lane(shape):
        return lax.broadcasted_iota(jnp.int32, shape, 1)

    def row(shape):
        return lax.broadcasted_iota(jnp.int32, shape, 0)

    for j in range(total):
        place = order_ref[j]
        xs[place] = in_ref[j // blocks, 0, j % blocks]
        seq[place] = in_ref[j // blocks, 1, j % blocks].astype(f32)
    chunk = lane((part, rows)) // fine
    for v in range(2):
        for g in range(groups):
            tiles = []
            for i in range(coarse):
                k = g * coarse + i
                t = xs[k] if v == 0 else in_ref[k // blocks, 2, k % blocks]
                tiles.append(t.astype(f32))
            d = 1
            while d < coarse:
                odd = (chunk // d) % 2 == 1
                for i in range(coarse):
                    if (i // d) % 2 == 0:
                        a, b = tiles[i], tiles[i + d]
                        tiles[i] = jnp.where(odd, pltpu.roll(b, fine * d, 1), a)
                        tiles[i + d] = jnp.where(odd, b, pltpu.roll(a, rows - fine * d, 1))
                d *= 2
            for e in range(coarse):
                ub[v, e, g] = tiles[e]
    upper = lane((fine, rows)) >= row((fine, rows))
    stair = lane((coarse, rows)) >= fine * row((coarse, rows))
    lanes = lane((fine, rows))
    last = row((2 * fine, rows)) == 2 * fine - 1
    def prepare(c, slot):
        def slanted(k):
            line = jnp.broadcast_to(seq[k, pl.ds(c, 1), :], (fine, rows)).astype(bf16)
            return pltpu.roll(line, 0, 1, stride=1, stride_axis=0)
        now = slanted(0)
        for k in range(total):
            after = slanted(k + 1) if k + 1 < total else jnp.zeros((fine, rows), bf16)
            wbuf[slot, k * fine : (k + 1) * fine, :] = jnp.where(upper, now, after)
            now = after
        for e in range(coarse):
            for v in range(2):
                before = jnp.zeros((coarse, rows), f32)
                shifted = [before]
                for g in range(groups):
                    line = jnp.broadcast_to(ub[v, e, g, pl.ds(c, 1), :], (coarse, rows))
                    turned = pltpu.roll(line, 0, 1, stride=fine, stride_axis=0)
                    shifted.append(jnp.where(stair, turned, before))
                    before = turned
                at = (2 * e + v) * fine
                for g in range(groups):
                    abuf[slot, at : at + fine, g * rows : (g + 1) * rows] = jnp.concatenate([shifted[g + 1], shifted[g]], axis=0).astype(bf16)
    def finish(c, slot):
        half_k = total // 2 * fine
        w1 = wbuf[slot, half_k:, :]
        first = jnp.dot(
            abuf[slot, :, : 2 * rows],
            jnp.concatenate([wbuf[slot, :half_k, :], w1], axis=1),
            preferred_element_type=f32,
        )
        second = jnp.dot(abuf[slot, :, 2 * rows :], w1, preferred_element_type=f32)
        low = first[:, :rows] + second
        high = first[:, rows:]
        for v in range(2):
            halves = []
            for half in (low, high):
                straight = half[v * fine : (v + 1) * fine]
                wrapped = jnp.zeros((fine, rows), f32)
                for e in range(1, coarse):
                    at = (2 * e + v) * fine
                    turned = pltpu.roll(half[at : at + fine], fine * e, 1)
                    keep = jnp.where(lanes >= fine * e, turned, 0.0)
                    straight += keep
                    wrapped += turned - keep
                halves.append((straight, wrapped))
            straight = jnp.concatenate([h[0] for h in halves], axis=0)
            wrapped = jnp.concatenate([h[1] for h in halves], axis=0)
            wrapped = jnp.where(last, 0.0, pltpu.roll(wrapped, 2 * fine - 1, 0))
            res[c, v * total : (v + 1) * total] = straight + wrapped

    def body(i, carry):
        for u in range(UNROLL):
            prepare(i * UNROLL + u, u)
        for u in range(UNROLL):
            finish(i * UNROLL + u, u)
        return carry

    lax.fori_loop(0, part // UNROLL, body, 0)
    results = res.reshape(part * 2 * total, rows)
    for j in range(total):
        place = order_ref[j]
        value = results[pl.ds(j, part, stride=2 * total), :]
        dx = results[pl.ds(total + place, part, stride=2 * total), :]
        value = value * CODE_SCALE
        out_ref[j // blocks, 0, j % blocks] = (value * value * value).astype(bf16)
        out_ref[j // blocks, 1, j % blocks] = dx.astype(bf16)


def per_device(x_groups, grad_groups, filters, group_order):
    blocks, rows, channels = x_groups.shape
    peers = lax.axis_size("seq")
    part = channels // peers
    total = peers * blocks
    vmem = pl.BlockSpec(memory_space=pltpu.VMEM)
    smem = pl.BlockSpec(memory_space=pltpu.SMEM)
    params = pltpu.CompilerParams(vmem_limit_bytes=VMEM_LIMIT)
    packed = jax.ShapeDtypeStruct((peers, 3, blocks, part, rows), jnp.bfloat16)
    coded = jax.ShapeDtypeStruct((peers, 2, blocks, part, rows), jnp.bfloat16)
    send = pl.pallas_call(
        pack_kernel,
        out_shape=packed,
        in_specs=[pl.BlockSpec(memory_space=pl.ANY)] * 3,
        out_specs=vmem,
        scratch_shapes=[
            pltpu.VMEM((blocks, rows, channels), jnp.bfloat16),
            pltpu.VMEM((blocks, rows, channels), jnp.bfloat16),
            pltpu.VMEM((blocks * rows, channels), jnp.bfloat16),
            pltpu.SemaphoreType.DMA((3,)),
        ],
    )(x_groups, grad_groups, filters)
    got = lax.all_to_all(send, "seq", 0, 0, tiled=True)
    back = pl.pallas_call(
        conv_kernel,
        out_shape=coded,
        in_specs=[smem, vmem],
        out_specs=vmem,
        scratch_shapes=[
            pltpu.VMEM((total, part, rows), jnp.bfloat16),
            pltpu.VMEM((total + 1, part, rows), jnp.float32),
            pltpu.VMEM((2, rows // 16, total * 16 // rows, part, rows), jnp.float32),
            pltpu.VMEM((part, 2 * total, rows), jnp.float32),
            pltpu.VMEM((UNROLL, 16 * total, rows), jnp.bfloat16),
            pltpu.VMEM((UNROLL, 2 * rows, 16 * total), jnp.bfloat16),
        ],
        compiler_params=params,
    )(group_order, got)
    home = lax.all_to_all(back, "seq", 0, 0, tiled=True)
    grad_x, grad_filters = pl.pallas_call(
        unpack_kernel,
        out_shape=(
            jax.ShapeDtypeStruct((blocks, rows, channels), jnp.bfloat16),
            jax.ShapeDtypeStruct((blocks * rows, channels), jnp.float32),
        ),
        in_specs=[vmem],
        out_specs=(vmem, vmem),
        compiler_params=params,
    )(home)
    return grad_x, grad_filters


def solution(mesh):
    placed = (P("seq", None, "chan"), P("seq", None, "chan"), P("seq", "chan"), P())
    return jax.shard_map(
        per_device,
        mesh=mesh,
        in_specs=placed,
        out_specs=(P("seq", None, "chan"), P("seq", "chan")),
        check_vma=False,
    )
```

profile of v0, /device:TPU:1, one launch (start us, length us, event | category | flops | bytes accessed | tf_op | source)
XLA Modules:
  0.0 46.4 jit_solution(9230046684279982457)
XLA Ops:
  0.6 2.1 %shard_map.59 = bf16[16,3,2,16,128]{4,3,2,1,0:T(8,128)(2,1)} custom-call(bf16[2,128,256]{2,1,0:T(8,128)(2,1)} %x_hbm.1, bf16[2,128,256]{2,1,0:T(8,128)(2,1)} %g_hbm.1, bf16[256,256]{1,0:T(8,128)(2,1)} %h_hbm.1), custom_call_target="tpu_custom_call" | custom-call | tf_op jit(solution)/shard_map/pallas_call | solution.py:187
  2.7 0.0 copy-start
  2.7 24.5 %all_to_all.10.in_ref = bf16[16,3,2,16,128]{4,3,2,1,0:T(8,128)(2,1)S(1)} all-to-all(bf16[16,3,2,16,128]{4,3,2,1,0:T(8,128)(2,1)} %shard_map.59), channel_id=1, replica_groups=mesh['seq'=16,'chan'=16] {'seq'}, dimensions={0} | all-to-all | bytes 786432 | tf_op jit(solution)/shard_map/all_to_all | solution.py:199
  27.2 0.0 copy-done
  27.2 3.8 %shard_map.60 = bf16[16,2,2,16,128]{4,3,2,1,0:T(8,128)(2,1)S(1)} custom-call(s32[32]{0:T(128)S(1)} %copy-done, bf16[16,3,2,16,128]{4,3,2,1,0:T(8,128)(2,1)S(1)} %all_to_all.10.in_ref), custom_call_target="tpu_custom_call" | custom-call | tf_op jit(solution)/shard_map/pallas_call | solution.py:200
  31.0 14.4 %all_to_all.11.in_ref = bf16[16,2,2,16,128]{4,3,2,1,0:T(8,128)(2,1)S(1)} all-to-all(bf16[16,2,2,16,128]{4,3,2,1,0:T(8,128)(2,1)S(1)} %shard_map.60), channel_id=1, replica_groups=mesh['seq'=16,'chan'=16] {'seq'}, dimensions={0} | all-to-all | bytes 524288 | tf_op jit(solution)/shard_map/all_to_all | solution.py:215
  45.4 1.0 %shard_map.61 = (bf16[2,128,256]{2,1,0:T(8,128)(2,1)}, f32[256,256]{1,0:T(8,128)}) custom-call(bf16[16,2,2,16,128]{4,3,2,1,0:T(8,128)(2,1)S(1)} %all_to_all.11.in_ref), custom_call_target="tpu_custom_call" | custom-call | tf_op jit(solution)/shard_map/pallas_call | solution.py:216
Async XLA Ops:
  2.7 24.5 %copy-start = (s32[32]{0:T(128)S(1)}, s32[32]{0:T(128)}, u32[]{:S(2)}) copy-start(s32[32]{0:T(128)} %order_ref.1) | copy-start | bytes 388
where the time goes:
time: 46.6 us; the launch traced here: 46.4 us
  blocking collectives  38.9 us (83%)
  Pallas kernels  6.84 us (15%)
  between operations  0.65 us (1%)
    all_to_all x1, blocking collectives, per_device(): got = lax.all_to_all(send, 'seq', 0, 0, tiled=True)  24.5 us
    all_to_all x1, blocking collectives, per_device(): home = lax.all_to_all(back, 'seq', 0, 0, tiled=True)  14.4 us
    pallas_call x1, Pallas kernels, per_device(): pl.pallas_call(conv_kernel, out_shape=coded, in_specs=[smem, vmem], out_s...  3.79 us
    pallas_call x1, Pallas kernels, per_device(): pl.pallas_call(pack_kernel, out_shape=packed, in_specs=[pl.BlockSpec(memo...  2.06 us
    pallas_call x1, Pallas kernels, per_device(): pl.pallas_call(unpack_kernel, out_shape=(jax.ShapeDtypeStruct((blocks, ro...  1 us

commit v1 on v0

--- a/solution.py
+++ b/solution.py
@@ -8,7 +8,7 @@
 from jax.sharding import PartitionSpec as P
 
 VMEM_LIMIT = 48 * 1024 * 1024
-UNROLL = 8
+UNROLL = 16
 CODE_SCALE = 2.0**30
 
 
@@ -66,10 +66,12 @@
         gx_ref[b] = transposed(eye, dx).astype(jnp.bfloat16)
 
 
-def conv_kernel(order_ref, in_ref, out_ref, xs, seq, ub, res, wbuf, abuf):
+def conv_kernel(order_any, in_ref, out_ref, xs, seq, ub, res, wbuf, abuf, order_ref, order_sem):
     f32, bf16 = jnp.float32, jnp.bfloat16
     peers, _, blocks, part, rows = in_ref.shape
     total = peers * blocks
+    order_copy = pltpu.make_async_copy(order_any, order_ref, order_sem)
+    order_copy.start()
     fine = 16
     coarse = rows // fine
     groups = total // coarse
@@ -80,12 +82,8 @@
     def row(shape):
         return lax.broadcasted_iota(jnp.int32, shape, 0)
 
-    for j in range(total):
-        place = order_ref[j]
-        xs[place] = in_ref[j // blocks, 0, j % blocks]
-        seq[place] = in_ref[j // blocks, 1, j % blocks].astype(f32)
     chunk = lane((part, rows)) // fine
-    for v in range(2):
+    def regroup(v):
         for g in range(groups):
             tiles = []
             for i in range(coarse):
@@ -107,7 +105,7 @@
     stair = lane((coarse, rows)) >= fine * row((coarse, rows))
     lanes = lane((fine, rows))
     last = row((2 * fine, rows)) == 2 * fine - 1
-    def prepare(c, slot):
+    def prepare_right(c, slot):
         def slanted(k):
             line = jnp.broadcast_to(seq[k, pl.ds(c, 1), :], (fine, rows)).astype(bf16)
             return pltpu.roll(line, 0, 1, stride=1, stride_axis=0)
@@ -116,18 +114,18 @@
             after = slanted(k + 1) if k + 1 < total else jnp.zeros((fine, rows), bf16)
             wbuf[slot, k * fine : (k + 1) * fine, :] = jnp.where(upper, now, after)
             now = after
+    def prepare_left(c, slot, v):
         for e in range(coarse):
-            for v in range(2):
-                before = jnp.zeros((coarse, rows), f32)
-                shifted = [before]
-                for g in range(groups):
-                    line = jnp.broadcast_to(ub[v, e, g, pl.ds(c, 1), :], (coarse, rows))
-                    turned = pltpu.roll(line, 0, 1, stride=fine, stride_axis=0)
-                    shifted.append(jnp.where(stair, turned, before))
-                    before = turned
-                at = (2 * e + v) * fine
-                for g in range(groups):
-                    abuf[slot, at : at + fine, g * rows : (g + 1) * rows] = jnp.concatenate([shifted[g + 1], shifted[g]], axis=0).astype(bf16)
+            before = jnp.zeros((coarse, rows), f32)
+            shifted = [before]
+            for g in range(groups):
+                line = jnp.broadcast_to(ub[v, e, g, pl.ds(c, 1), :], (coarse, rows))
+                turned = pltpu.roll(line, 0, 1, stride=fine, stride_axis=0)
+                shifted.append(jnp.where(stair, turned, before))
+                before = turned
+            at = (2 * e + v) * fine
+            for g in range(groups):
+                abuf[slot, at : at + fine, g * rows : (g + 1) * rows] = jnp.concatenate([shifted[g + 1], shifted[g]], axis=0).astype(bf16)
     def finish(c, slot):
         half_k = total // 2 * fine
         w1 = wbuf[slot, half_k:, :]
@@ -156,14 +154,23 @@
             wrapped = jnp.where(last, 0.0, pltpu.roll(wrapped, 2 * fine - 1, 0))
             res[c, v * total : (v + 1) * total] = straight + wrapped
 
-    def body(i, carry):
+    regroup(1)
+    for u in range(UNROLL):
+        prepare_left(u, u, 1)
+    order_copy.wait()
+    for j in range(total):
+        place = order_ref[j]
+        xs[place] = in_ref[j // blocks, 0, j % blocks]
+        seq[place] = in_ref[j // blocks, 1, j % blocks].astype(f32)
+    regroup(0)
+    for first in range(0, part, UNROLL):
         for u in range(UNROLL):
-            prepare(i * UNROLL + u, u)
+            prepare_right(first + u, u)
+            prepare_left(first + u, u, 0)
+            if first:
+                prepare_left(first + u, u, 1)
         for u in range(UNROLL):
-            finish(i * UNROLL + u, u)
-        return carry
-
-    lax.fori_loop(0, part // UNROLL, body, 0)
+            finish(first + u, u)
     results = res.reshape(part * 2 * total, rows)
     for j in range(total):
         place = order_ref[j]
@@ -180,7 +187,6 @@
     part = channels // peers
     total = peers * blocks
     vmem = pl.BlockSpec(memory_space=pltpu.VMEM)
-    smem = pl.BlockSpec(memory_space=pltpu.SMEM)
     params = pltpu.CompilerParams(vmem_limit_bytes=VMEM_LIMIT)
     packed = jax.ShapeDtypeStruct((peers, 3, blocks, part, rows), jnp.bfloat16)
     coded = jax.ShapeDtypeStruct((peers, 2, blocks, part, rows), jnp.bfloat16)
@@ -200,7 +206,7 @@
     back = pl.pallas_call(
         conv_kernel,
         out_shape=coded,
-        in_specs=[smem, vmem],
+        in_specs=[pl.BlockSpec(memory_space=pl.ANY), vmem],
         out_specs=vmem,
         scratch_shapes=[
             pltpu.VMEM((total, part, rows), jnp.bfloat16),
@@ -209,6 +215,8 @@
             pltpu.VMEM((part, 2 * total, rows), jnp.float32),
             pltpu.VMEM((UNROLL, 16 * total, rows), jnp.bfloat16),
             pltpu.VMEM((UNROLL, 2 * rows, 16 * total), jnp.bfloat16),
+            pltpu.SMEM((total,), jnp.int32),
+            pltpu.SemaphoreType.DMA,
         ],
         compiler_params=params,
     )(group_order, got)

time: 46.6 us -> 46 us (0.987)
  Pallas kernels: 6.84 us -> 6.17 us
    pallas_call x1, Pallas kernels: 3.79 us -> 3.11 us  [per_device(): pl.pallas_call(conv_kernel, out_shape=coded, in_specs=[pl.BlockSpec(memor...]
where the time goes in v1:
time: 46 us; the launch traced here: 45.7 us
  blocking collectives  38.9 us (85%)
  Pallas kernels  6.17 us (13%)
  between operations  0.66 us (1%)
    all_to_all x1, blocking collectives, per_device(): got = lax.all_to_all(send, 'seq', 0, 0, tiled=True)  24.5 us
    all_to_all x1, blocking collectives, per_device(): home = lax.all_to_all(back, 'seq', 0, 0, tiled=True)  14.4 us
    pallas_call x1, Pallas kernels, per_device(): pl.pallas_call(conv_kernel, out_shape=coded, in_specs=[pl.BlockSpec(memor...  3.11 us
    pallas_call x1, Pallas kernels, per_device(): pl.pallas_call(pack_kernel, out_shape=packed, in_specs=[pl.BlockSpec(memo...  2.06 us
    pallas_call x1, Pallas kernels, per_device(): pl.pallas_call(unpack_kernel, out_shape=(jax.ShapeDtypeStruct((blocks, ro...  1 us

profile of v1, /device:TPU:1, one launch (start us, length us, event | category | flops | bytes accessed | tf_op | source)
XLA Modules:
  0.0 45.7 jit_solution(2759327023739038428)
XLA Ops:
  0.6 2.1 %shard_map.59 = bf16[16,3,2,16,128]{4,3,2,1,0:T(8,128)(2,1)} custom-call(bf16[2,128,256]{2,1,0:T(8,128)(2,1)} %x_hbm.1, bf16[2,128,256]{2,1,0:T(8,128)(2,1)} %g_hbm.1, bf16[256,256]{1,0:T(8,128)(2,1)} %h_hbm.1), custom_call_target="tpu_custom_call" | custom-call | tf_op jit(solution)/shard_map/pallas_call | solution.py:193
  2.7 0.0 copy-start
  2.7 24.5 %all_to_all.10.in_ref = bf16[16,3,2,16,128]{4,3,2,1,0:T(8,128)(2,1)S(1)} all-to-all(bf16[16,3,2,16,128]{4,3,2,1,0:T(8,128)(2,1)} %shard_map.59), channel_id=1, replica_groups=mesh['seq'=16,'chan'=16] {'seq'}, dimensions={0} | all-to-all | bytes 786432 | tf_op jit(solution)/shard_map/all_to_all | solution.py:205
  27.2 0.0 copy-done
  27.2 3.1 %shard_map.60 = bf16[16,2,2,16,128]{4,3,2,1,0:T(8,128)(2,1)S(1)} custom-call(s32[32]{0:T(128)S(1)} %copy-done, bf16[16,3,2,16,128]{4,3,2,1,0:T(8,128)(2,1)S(1)} %all_to_all.10.in_ref), custom_call_target="tpu_custom_call" | custom-call | tf_op jit(solution)/shard_map/pallas_call | solution.py:206
  30.4 14.4 %all_to_all.11.in_ref = bf16[16,2,2,16,128]{4,3,2,1,0:T(8,128)(2,1)S(1)} all-to-all(bf16[16,2,2,16,128]{4,3,2,1,0:T(8,128)(2,1)S(1)} %shard_map.60), channel_id=1, replica_groups=mesh['seq'=16,'chan'=16] {'seq'}, dimensions={0} | all-to-all | bytes 524288 | tf_op jit(solution)/shard_map/all_to_all | solution.py:223
  44.7 1.0 %shard_map.61 = (bf16[2,128,256]{2,1,0:T(8,128)(2,1)}, f32[256,256]{1,0:T(8,128)}) custom-call(bf16[16,2,2,16,128]{4,3,2,1,0:T(8,128)(2,1)S(1)} %all_to_all.11.in_ref), custom_call_target="tpu_custom_call" | custom-call | tf_op jit(solution)/shard_map/pallas_call | solution.py:224
Async XLA Ops:
  2.7 24.5 %copy-start = (s32[32]{0:T(128)S(1)}, s32[32]{0:T(128)}, u32[]{:S(2)}) copy-start(s32[32]{0:T(128)} %order_any.1) | copy-start | bytes 388

commit v2 on v1

--- a/solution.py
+++ b/solution.py
@@ -37,14 +37,13 @@
     ]
     for copy in copies:
         copy.start()
-    flip = permuter(rows, True)
 
     def put(a, b, value):
         out_ref[:, a, b] = value.astype(jnp.bfloat16).reshape(peers, part, rows)
 
     copies[0].wait()
     for b in range(blocks):
-        put(1, b, jnp.dot(g_ref[b].T, flip, preferred_element_type=jnp.float32))
+        put(1, b, g_ref[b].T)
     copies[1].wait()
     for b in range(blocks):
         put(0, b, x_ref[b].T)
@@ -157,11 +156,14 @@
     regroup(1)
     for u in range(UNROLL):
         prepare_left(u, u, 1)
+    flip = permuter(rows, True)
+    grads = in_ref[:, 1].reshape(total * part, rows)
+    flipped = jnp.dot(grads, flip, preferred_element_type=f32)
     order_copy.wait()
     for j in range(total):
         place = order_ref[j]
         xs[place] = in_ref[j // blocks, 0, j % blocks]
-        seq[place] = in_ref[j // blocks, 1, j % blocks].astype(f32)
+        seq[place] = flipped[j * part : (j + 1) * part]
     regroup(0)
     for first in range(0, part, UNROLL):
         for u in range(UNROLL):

time: 46 us -> 45.8 us (level)
  no operation moved by 1% of the time
where the time goes in v2:
time: 45.8 us; the launch traced here: 45.6 us
  blocking collectives  38.9 us (85%)
  Pallas kernels  6.05 us (13%)
  between operations  0.66 us (1%)
    all_to_all x1, blocking collectives, per_device(): got = lax.all_to_all(send, 'seq', 0, 0, tiled=True)  24.5 us
    all_to_all x1, blocking collectives, per_device(): home = lax.all_to_all(back, 'seq', 0, 0, tiled=True)  14.4 us
    pallas_call x1, Pallas kernels, per_device(): pl.pallas_call(conv_kernel, out_shape=coded, in_specs=[pl.BlockSpec(memor...  3.12 us
    pallas_call x1, Pallas kernels, per_device(): pl.pallas_call(pack_kernel, out_shape=packed, in_specs=[pl.BlockSpec(memo...  1.93 us
    pallas_call x1, Pallas kernels, per_device(): pl.pallas_call(unpack_kernel, out_shape=(jax.ShapeDtypeStruct((blocks, ro...  1 us

profile of v2, /device:TPU:1, one launch (start us, length us, event | category | flops | bytes accessed | tf_op | source)
XLA Modules:
  0.0 45.6 jit_solution(2551366864624754303)
XLA Ops:
  0.6 1.9 %shard_map.59 = bf16[16,3,2,16,128]{4,3,2,1,0:T(8,128)(2,1)} custom-call(bf16[2,128,256]{2,1,0:T(8,128)(2,1)} %x_hbm.1, bf16[2,128,256]{2,1,0:T(8,128)(2,1)} %g_hbm.1, bf16[256,256]{1,0:T(8,128)(2,1)} %h_hbm.1), custom_call_target="tpu_custom_call" | custom-call | tf_op jit(solution)/shard_map/pallas_call | solution.py:195
  2.6 0.0 copy-start
  2.6 24.5 %all_to_all.10.in_ref = bf16[16,3,2,16,128]{4,3,2,1,0:T(8,128)(2,1)S(1)} all-to-all(bf16[16,3,2,16,128]{4,3,2,1,0:T(8,128)(2,1)} %shard_map.59), channel_id=1, replica_groups=mesh['seq'=16,'chan'=16] {'seq'}, dimensions={0} | all-to-all | bytes 786432 | tf_op jit(solution)/shard_map/all_to_all | solution.py:207
  27.1 0.0 copy-done
  27.1 3.1 %shard_map.60 = bf16[16,2,2,16,128]{4,3,2,1,0:T(8,128)(2,1)S(1)} custom-call(s32[32]{0:T(128)S(1)} %copy-done, bf16[16,3,2,16,128]{4,3,2,1,0:T(8,128)(2,1)S(1)} %all_to_all.10.in_ref), custom_call_target="tpu_custom_call" | custom-call | tf_op jit(solution)/shard_map/pallas_call | solution.py:208
  30.2 14.4 %all_to_all.11.in_ref = bf16[16,2,2,16,128]{4,3,2,1,0:T(8,128)(2,1)S(1)} all-to-all(bf16[16,2,2,16,128]{4,3,2,1,0:T(8,128)(2,1)S(1)} %shard_map.60), channel_id=1, replica_groups=mesh['seq'=16,'chan'=16] {'seq'}, dimensions={0} | all-to-all | bytes 524288 | tf_op jit(solution)/shard_map/all_to_all | solution.py:225
  44.6 1.0 %shard_map.61 = (bf16[2,128,256]{2,1,0:T(8,128)(2,1)}, f32[256,256]{1,0:T(8,128)}) custom-call(bf16[16,2,2,16,128]{4,3,2,1,0:T(8,128)(2,1)S(1)} %all_to_all.11.in_ref), custom_call_target="tpu_custom_call" | custom-call | tf_op jit(solution)/shard_map/pallas_call | solution.py:226
Async XLA Ops:
  2.6 24.6 %copy-start = (s32[32]{0:T(128)S(1)}, s32[32]{0:T(128)}, u32[]{:S(2)}) copy-start(s32[32]{0:T(128)} %order_any.1) | copy-start | bytes 388

commit v3 on v2

--- a/solution.py
+++ b/solution.py
@@ -88,7 +88,7 @@
             for i in range(coarse):
                 k = g * coarse + i
                 t = xs[k] if v == 0 else in_ref[k // blocks, 2, k % blocks]
-                tiles.append(t.astype(f32))
+                tiles.append(t)
             d = 1
             while d < coarse:
                 odd = (chunk // d) % 2 == 1
@@ -99,7 +99,7 @@
                         tiles[i + d] = jnp.where(odd, b, pltpu.roll(a, rows - fine * d, 1))
                 d *= 2
             for e in range(coarse):
-                ub[v, e, g] = tiles[e]
+                ub[v, e, g] = tiles[e].astype(f32)
     upper = lane((fine, rows)) >= row((fine, rows))
     stair = lane((coarse, rows)) >= fine * row((coarse, rows))
     lanes = lane((fine, rows))

time: 45.8 us -> 45.8 us (level)
  no operation moved by 1% of the time
where the time goes in v3:
time: 45.8 us; the launch traced here: 45.6 us
  blocking collectives  38.9 us (85%)
  Pallas kernels  6.05 us (13%)
  between operations  0.66 us (1%)
    all_to_all x1, blocking collectives, per_device(): got = lax.all_to_all(send, 'seq', 0, 0, tiled=True)  24.5 us
    all_to_all x1, blocking collectives, per_device(): home = lax.all_to_all(back, 'seq', 0, 0, tiled=True)  14.4 us
    pallas_call x1, Pallas kernels, per_device(): pl.pallas_call(conv_kernel, out_shape=coded, in_specs=[pl.BlockSpec(memor...  3.12 us
    pallas_call x1, Pallas kernels, per_device(): pl.pallas_call(pack_kernel, out_shape=packed, in_specs=[pl.BlockSpec(memo...  1.93 us
    pallas_call x1, Pallas kernels, per_device(): pl.pallas_call(unpack_kernel, out_shape=(jax.ShapeDtypeStruct((blocks, ro...  1 us

profile of v3, /device:TPU:1, one launch (start us, length us, event | category | flops | bytes accessed | tf_op | source)
XLA Modules:
  0.0 45.6 jit_solution(8987864458718615820)
XLA Ops:
  0.6 1.9 %shard_map.59 = bf16[16,3,2,16,128]{4,3,2,1,0:T(8,128)(2,1)} custom-call(bf16[2,128,256]{2,1,0:T(8,128)(2,1)} %x_hbm.1, bf16[2,128,256]{2,1,0:T(8,128)(2,1)} %g_hbm.1, bf16[256,256]{1,0:T(8,128)(2,1)} %h_hbm.1), custom_call_target="tpu_custom_call" | custom-call | tf_op jit(solution)/shard_map/pallas_call | solution.py:195
  2.6 0.0 copy-start
  2.6 24.5 %all_to_all.10.in_ref = bf16[16,3,2,16,128]{4,3,2,1,0:T(8,128)(2,1)S(1)} all-to-all(bf16[16,3,2,16,128]{4,3,2,1,0:T(8,128)(2,1)} %shard_map.59), channel_id=1, replica_groups=mesh['seq'=16,'chan'=16] {'seq'}, dimensions={0} | all-to-all | bytes 786432 | tf_op jit(solution)/shard_map/all_to_all | solution.py:207
  27.1 0.0 copy-done
  27.1 3.1 %shard_map.60 = bf16[16,2,2,16,128]{4,3,2,1,0:T(8,128)(2,1)S(1)} custom-call(s32[32]{0:T(128)S(1)} %copy-done, bf16[16,3,2,16,128]{4,3,2,1,0:T(8,128)(2,1)S(1)} %all_to_all.10.in_ref), custom_call_target="tpu_custom_call" | custom-call | tf_op jit(solution)/shard_map/pallas_call | solution.py:208
  30.2 14.4 %all_to_all.11.in_ref = bf16[16,2,2,16,128]{4,3,2,1,0:T(8,128)(2,1)S(1)} all-to-all(bf16[16,2,2,16,128]{4,3,2,1,0:T(8,128)(2,1)S(1)} %shard_map.60), channel_id=1, replica_groups=mesh['seq'=16,'chan'=16] {'seq'}, dimensions={0} | all-to-all | bytes 524288 | tf_op jit(solution)/shard_map/all_to_all | solution.py:225
  44.6 1.0 %shard_map.61 = (bf16[2,128,256]{2,1,0:T(8,128)(2,1)}, f32[256,256]{1,0:T(8,128)}) custom-call(bf16[16,2,2,16,128]{4,3,2,1,0:T(8,128)(2,1)S(1)} %all_to_all.11.in_ref), custom_call_target="tpu_custom_call" | custom-call | tf_op jit(solution)/shard_map/pallas_call | solution.py:226
Async XLA Ops:
  2.6 24.6 %copy-start = (s32[32]{0:T(128)S(1)}, s32[32]{0:T(128)}, u32[]{:S(2)}) copy-start(s32[32]{0:T(128)} %order_any.1) | copy-start | bytes 388

commit v4 on v2

--- a/solution.py
+++ b/solution.py
@@ -21,9 +21,7 @@
 
 
 def transposed(eye, value):
-    return lax.dot_general(
-        eye, value, (((1,), (1,)), ((), ())), preferred_element_type=jnp.float32
-    )
+    return jnp.dot(eye, value.T, preferred_element_type=jnp.float32)
 
 
 def pack_kernel(x_hbm, g_hbm, h_hbm, out_ref, x_ref, g_ref, h_ref, sems):

time: 45.8 us -> 45.8 us (level)
  no operation moved by 1% of the time
where the time goes in v4:
time: 45.8 us; the launch traced here: 45.6 us
  blocking collectives  38.9 us (85%)
  Pallas kernels  6.05 us (13%)
  between operations  0.66 us (1%)
    all_to_all x1, blocking collectives, per_device(): got = lax.all_to_all(send, 'seq', 0, 0, tiled=True)  24.5 us
    all_to_all x1, blocking collectives, per_device(): home = lax.all_to_all(back, 'seq', 0, 0, tiled=True)  14.4 us
    pallas_call x1, Pallas kernels, per_device(): pl.pallas_call(conv_kernel, out_shape=coded, in_specs=[pl.BlockSpec(memor...  3.13 us
    pallas_call x1, Pallas kernels, per_device(): pl.pallas_call(pack_kernel, out_shape=packed, in_specs=[pl.BlockSpec(memo...  1.93 us
    pallas_call x1, Pallas kernels, per_device(): pl.pallas_call(unpack_kernel, out_shape=(jax.ShapeDtypeStruct((blocks, ro...  1 us

profile of v4, /device:TPU:1, one launch (start us, length us, event | category | flops | bytes accessed | tf_op | source)
XLA Modules:
  0.0 45.6 jit_solution(2551366864624754303)
XLA Ops:
  0.6 1.9 %shard_map.59 = bf16[16,3,2,16,128]{4,3,2,1,0:T(8,128)(2,1)} custom-call(bf16[2,128,256]{2,1,0:T(8,128)(2,1)} %x_hbm.1, bf16[2,128,256]{2,1,0:T(8,128)(2,1)} %g_hbm.1, bf16[256,256]{1,0:T(8,128)(2,1)} %h_hbm.1), custom_call_target="tpu_custom_call" | custom-call | tf_op jit(solution)/shard_map/pallas_call | solution.py:193
  2.6 0.0 copy-start
  2.6 24.5 %all_to_all.10.in_ref = bf16[16,3,2,16,128]{4,3,2,1,0:T(8,128)(2,1)S(1)} all-to-all(bf16[16,3,2,16,128]{4,3,2,1,0:T(8,128)(2,1)} %shard_map.59), channel_id=1, replica_groups=mesh['seq'=16,'chan'=16] {'seq'}, dimensions={0} | all-to-all | bytes 786432 | tf_op jit(solution)/shard_map/all_to_all | solution.py:205
  27.1 0.0 copy-done
  27.1 3.1 %shard_map.60 = bf16[16,2,2,16,128]{4,3,2,1,0:T(8,128)(2,1)S(1)} custom-call(s32[32]{0:T(128)S(1)} %copy-done, bf16[16,3,2,16,128]{4,3,2,1,0:T(8,128)(2,1)S(1)} %all_to_all.10.in_ref), custom_call_target="tpu_custom_call" | custom-call | tf_op jit(solution)/shard_map/pallas_call | solution.py:206
  30.2 14.4 %all_to_all.11.in_ref = bf16[16,2,2,16,128]{4,3,2,1,0:T(8,128)(2,1)S(1)} all-to-all(bf16[16,2,2,16,128]{4,3,2,1,0:T(8,128)(2,1)S(1)} %shard_map.60), channel_id=1, replica_groups=mesh['seq'=16,'chan'=16] {'seq'}, dimensions={0} | all-to-all | bytes 524288 | tf_op jit(solution)/shard_map/all_to_all | solution.py:223
  44.6 1.0 %shard_map.61 = (bf16[2,128,256]{2,1,0:T(8,128)(2,1)}, f32[256,256]{1,0:T(8,128)}) custom-call(bf16[16,2,2,16,128]{4,3,2,1,0:T(8,128)(2,1)S(1)} %all_to_all.11.in_ref), custom_call_target="tpu_custom_call" | custom-call | tf_op jit(solution)/shard_map/pallas_call | solution.py:224
Async XLA Ops:
  2.6 24.6 %copy-start = (s32[32]{0:T(128)S(1)}, s32[32]{0:T(128)}, u32[]{:S(2)}) copy-start(s32[32]{0:T(128)} %order_any.1) | copy-start | bytes 388
